TPU v7x, 32 devices: a whole 2x2x4 slice. The times are simulated.
32 devices in a mesh: seq: 8 (over z, x), batch: 4 (over y, core).
Axes of the slice: x: 2, y: 2, z: 4, core: 2. Of those that a mesh axis runs over, the one named last changes fastest.
Arguments:
- inputs: bfloat16 [4, 1024, 768], P('batch', 'seq'), may hold values from -6 to 6
- cotangent: bfloat16 [4, 1024, 768], P('batch', 'seq'), may hold values from -6 to 6
- doc_lengths: int32 [4, 9], P('batch'), may hold values from 1 to 896, as said below
- gain_one: float32 [768], replicated, may hold values from 0.5 to 1.5
- shift_one: float32 [768], replicated, may hold values from -2 to 2
- qkv_weight: bfloat16 [768, 2304], replicated, may hold values from -0.21875 to 0.21875
- qkv_bias: float32 [2304], replicated, may hold values from -2 to 2
- proj_weight: bfloat16 [768, 768], replicated, may hold values from -6 to 6
- proj_bias: float32 [768], replicated, may hold values from -2 to 2
- gain_two: float32 [768], replicated, may hold values from 0.5 to 1.5
- shift_two: float32 [768], replicated, may hold values from -2 to 2
- up_weight: bfloat16 [768, 3072], replicated, may hold values from -0.21875 to 0.21875
- up_bias: float32 [3072], replicated, may hold values from -2 to 2
- down_weight: bfloat16 [3072, 768], replicated, may hold values from -0.109375 to 0.109375
- down_bias: float32 [768], replicated, may hold values from -2 to 2
Outputs:
- layer_out: bfloat16 [4, 1024, 768], P('batch', 'seq')
- input_grad: bfloat16 [4, 1024, 768], P('batch', 'seq')
- grad_gain_one: float32 [768], replicated
- grad_shift_one: float32 [768], replicated
- grad_qkv_weight: float32 [768, 2304], replicated
- grad_qkv_bias: float32 [2304], replicated
- grad_proj_weight: float32 [768, 768], replicated
- grad_proj_bias: float32 [768], replicated
- grad_gain_two: float32 [768], replicated
- grad_shift_two: float32 [768], replicated
- grad_up_weight: float32 [768, 3072], replicated
- grad_up_bias: float32 [3072], replicated
- grad_down_weight: float32 [3072, 768], replicated
- grad_down_bias: float32 [768], replicated
Inputs may be any that keep to these rules, and one draw needn't show every extreme that they name: `doc_lengths`: each row lists in order the lengths of the 9 documents packed into one stream: 8 short ones that hold 128 tokens together, and one of exactly 896 tokens with at least one short document before it and one after it.
All inputs are finite; a program needn't handle non-finite values.
Results may differ from a plain program's by a relative error of at most 0.018.
Values may be sent and summed in bfloat16 or wider, within the bound.
A program may use at most 256 MiB of HBM per device.

v0:
```python
import math
import jax
import jax.numpy as jnp
from jax import lax
from jax.sharding import PartitionSpec as P

HEADS = 12
HD = 64
norm_eps = 1e-05
masked_low = -1e30


def from_behind(shard, axis, by):
    peers = lax.axis_size(axis)
    pairs = [(i, i + by) for i in range(peers) if 0 <= i + by < peers]
    return lax.ppermute(shard, axis, pairs)


def shifted(block, axis, distance):
    devices = range(lax.axis_size(axis))
    route = [((i - distance) % len(devices), i) for i in devices]
    return lax.ppermute(block, axis, route)


def layer_norm(rows, gain, shift):
    center = rows - jnp.mean(rows, axis=-1, keepdims=True)
    spread = jnp.mean(center * center, axis=-1, keepdims=True)
    return center * lax.rsqrt(spread + norm_eps) * gain + shift


def gelu_tanh(value):
    return jax.nn.gelu(value, approximate=True)


def doc_of(ends, first, count):
    places = first + jnp.arange(count, dtype=jnp.int32)
    return jnp.sum((ends[None, :] <= places[:, None]).astype(jnp.int32), axis=1)


def scores_of(q_heads, k_heads, allowed):
    raw = jnp.einsum("qhd,khd->hqk", q_heads, k_heads, preferred_element_type=jnp.float32)
    return jnp.where(allowed[None], raw * (1.0 / math.sqrt(q_heads.shape[2])), 0.0)


def forward_part(state, q_heads, k_heads, v_heads, allowed):
    running, total, accum = state
    scores = scores_of(q_heads, k_heads, allowed)
    top = jnp.max(jnp.where(allowed[None], jnp.abs(scores), masked_low), axis=2)
    newer = jnp.maximum(running, top)
    plus = jnp.where(allowed[None], jnp.exp(scores - newer[:, :, None]), 0.0)
    minus = jnp.where(allowed[None], jnp.exp(-scores - newer[:, :, None]), 0.0)
    keep = jnp.exp(running - newer)
    total = total * keep + jnp.sum(plus + minus, axis=2)
    weights = (plus - minus).astype(jnp.bfloat16)
    accum = accum * keep[:, :, None] + jnp.einsum(
        "hqk,khd->hqd", weights, v_heads, preferred_element_type=jnp.float32
    )
    return (newer, total, accum)


def backward_part(q_heads, k_heads, v_heads, grad_out, log_total, delta, allowed):
    scale = 1.0 / math.sqrt(q_heads.shape[2])
    scores = scores_of(q_heads, k_heads, allowed)
    plus = jnp.where(allowed[None], jnp.exp(scores - log_total[:, :, None]), 0.0)
    minus = jnp.where(allowed[None], jnp.exp(-scores - log_total[:, :, None]), 0.0)
    signed = plus - minus
    along = jnp.einsum("qhd,khd->hqk", grad_out, v_heads, preferred_element_type=jnp.float32)
    dscore = (((plus + minus) * along - signed * delta[:, :, None]) * scale).astype(jnp.bfloat16)
    weights = signed.astype(jnp.bfloat16)
    grad_q = jnp.einsum("hqk,khd->qhd", dscore, k_heads, preferred_element_type=jnp.float32)
    grad_k = jnp.einsum("hqk,qhd->khd", dscore, q_heads, preferred_element_type=jnp.float32)
    grad_v = jnp.einsum("hqk,qhd->khd", weights, grad_out, preferred_element_type=jnp.float32)
    return (grad_q, grad_k, grad_v)


def forward_step(state, q_heads, k_heads, v_heads, allowed):
    return forward_part(state, q_heads, k_heads, v_heads, allowed)


def backward_step(q_heads, k_heads, v_heads, grad_out, log_total, delta, allowed):
    return backward_part(q_heads, k_heads, v_heads, grad_out, log_total, delta, allowed)


def per_device(
    inputs,
    cotangent,
    doc_lengths,
    gain_one,
    shift_one,
    qkv_weight,
    qkv_bias,
    proj_weight,
    proj_bias,
    gain_two,
    shift_two,
    up_weight,
    up_bias,
    down_weight,
    down_bias,
):
    rows = inputs.shape[1]
    width = inputs.shape[2]
    index = lax.axis_index("seq")
    count = lax.axis_size("seq")
    ends = jnp.cumsum(doc_lengths[0])
    q_place = index * rows + jnp.arange(rows, dtype=jnp.int32)
    q_doc = doc_of(ends, index * rows, rows)

    def heads(flat):
        return flat.reshape(flat.shape[0], HEADS, HD)

    x_rows = inputs[0].astype(jnp.float32)
    norm_one = layer_norm(x_rows, gain_one, shift_one).astype(jnp.bfloat16)
    mixed = (jnp.dot(norm_one, qkv_weight, preferred_element_type=jnp.float32) + qkv_bias).astype(
        jnp.bfloat16
    )
    q_flat = mixed[:, :width]
    k_flat = mixed[:, width : 2 * width]
    v_flat = mixed[:, 2 * width :]
    q_heads = heads(q_flat)

    def allowed_for(first, extent):
        k_place = first + jnp.arange(extent, dtype=jnp.int32)
        k_doc = doc_of(ends, first, extent)
        return (q_doc[:, None] == k_doc[None, :]) & (k_place[None, :] <= q_place[:, None])

    start_state = (
        jnp.full((HEADS, rows), masked_low, jnp.float32),
        jnp.zeros((HEADS, rows), jnp.float32),
        jnp.zeros((HEADS, rows, HD), jnp.float32),
    )
    state = start_state
    k_all = lax.all_gather(k_flat, "seq", axis=0, tiled=True)
    v_all = lax.all_gather(v_flat, "seq", axis=0, tiled=True)
    fold_extent = k_all.shape[0]
    number = fold_extent // rows

    def one(inner, block):
        offset = block * rows
        k_blk = lax.dynamic_slice_in_dim(k_all, offset, rows, 0)
        v_blk = lax.dynamic_slice_in_dim(v_all, offset, rows, 0)
        allowed = allowed_for(offset, rows)
        return (forward_step(inner, q_heads, heads(k_blk), heads(v_blk), allowed), None)

    state, unused = lax.scan(one, state, jnp.arange(number, dtype=jnp.int32))
    running, total, accum = state
    attn_heads = accum / total[:, :, None]
    attn32 = jnp.transpose(attn_heads, (1, 0, 2)).reshape(rows, width)
    attn = attn32.astype(jnp.bfloat16)
    resid = x_rows + jnp.dot(attn, proj_weight, preferred_element_type=jnp.float32) + proj_bias
    norm_two = layer_norm(resid, gain_two, shift_two).astype(jnp.bfloat16)
    hidden = jnp.dot(norm_two, up_weight, preferred_element_type=jnp.float32) + up_bias
    active = gelu_tanh(hidden).astype(jnp.bfloat16)
    result = resid + jnp.dot(active, down_weight, preferred_element_type=jnp.float32) + down_bias
    layer_out = result.astype(jnp.bfloat16)[None]
    grad_rows = cotangent[0]
    grad_down_weight = jnp.einsum(
        "tf,td->fd", active, grad_rows, preferred_element_type=jnp.float32
    )
    grad_down_bias = jnp.sum(grad_rows.astype(jnp.float32), axis=0)
    grad_active = jnp.dot(grad_rows, down_weight.T, preferred_element_type=jnp.float32)
    gelu_back = jax.vjp(gelu_tanh, hidden)[1]
    grad_hidden = gelu_back(grad_active)[0].astype(jnp.bfloat16)
    grad_up_weight = jnp.einsum(
        "td,tf->df", norm_two, grad_hidden, preferred_element_type=jnp.float32
    )
    grad_up_bias = jnp.sum(grad_hidden.astype(jnp.float32), axis=0)
    grad_norm_two = jnp.dot(grad_hidden, up_weight.T, preferred_element_type=jnp.float32)
    norm_two_back = jax.vjp(layer_norm, resid, gain_two, shift_two)[1]
    resid_part, grad_gain_two, grad_shift_two = norm_two_back(grad_norm_two)
    grad_resid = grad_rows.astype(jnp.float32) + resid_part
    grad_branch = grad_resid.astype(jnp.bfloat16)
    grad_proj_weight = jnp.einsum(
        "td,te->de", attn, grad_branch, preferred_element_type=jnp.float32
    )
    grad_proj_bias = jnp.sum(grad_branch.astype(jnp.float32), axis=0)
    grad_attn = jnp.dot(grad_branch, proj_weight.T, preferred_element_type=jnp.float32).astype(
        jnp.bfloat16
    )
    grad_out = heads(grad_attn)
    log_total = running + jnp.log(total)
    delta = jnp.einsum("qhd,hqd->hq", grad_out.astype(jnp.float32), attn_heads)

    def circle_step(step, carry):
        k_held, v_held, acc_k, acc_v, grad_q = carry
        source = jnp.remainder(index - step, count)
        allowed = allowed_for(source * rows, rows)
        part = backward_step(
            q_heads, heads(k_held), heads(v_held), grad_out, log_total, delta, allowed
        )
        grad_q = grad_q + part[0]
        acc_k = acc_k + part[1].reshape(rows, width)
        acc_v = acc_v + part[2].reshape(rows, width)
        k_held, v_held = from_behind((k_held, v_held), "seq", 1)
        acc_k, acc_v = (
            shifted(acc_k.astype(jnp.bfloat16), "seq", 1).astype(acc_k.dtype),
            shifted(acc_v.astype(jnp.bfloat16), "seq", 1).astype(acc_v.dtype),
        )
        return (k_held, v_held, acc_k, acc_v, grad_q)

    circle_start = (
        k_flat,
        v_flat,
        jnp.zeros((rows, width), jnp.float32),
        jnp.zeros((rows, width), jnp.float32),
        jnp.zeros((rows, HEADS, HD), jnp.float32),
    )
    unused_k, unused_v, grad_k, grad_v, grad_q = lax.fori_loop(0, count, circle_step, circle_start)
    grad_mixed = jnp.concatenate(
        [
            grad_q.reshape(rows, width).astype(jnp.bfloat16),
            grad_k.astype(jnp.bfloat16),
            grad_v.astype(jnp.bfloat16),
        ],
        axis=1,
    )
    grad_qkv_weight = jnp.einsum(
        "td,te->de", norm_one, grad_mixed, preferred_element_type=jnp.float32
    )
    grad_qkv_bias = jnp.sum(grad_mixed.astype(jnp.float32), axis=0)
    grad_norm_one = jnp.dot(grad_mixed, qkv_weight.T, preferred_element_type=jnp.float32)
    norm_one_back = jax.vjp(layer_norm, x_rows, gain_one, shift_one)[1]
    input_part, grad_gain_one, grad_shift_one = norm_one_back(grad_norm_one)
    input_grad = (grad_resid + input_part).astype(jnp.bfloat16)[None]
    members = (
        grad_gain_one,
        grad_shift_one,
        grad_qkv_weight,
        grad_qkv_bias,
        grad_proj_weight,
        grad_proj_bias,
        grad_gain_two,
        grad_shift_two,
        grad_up_weight,
        grad_up_bias,
        grad_down_weight,
        grad_down_bias,
    )
    joined = jnp.concatenate([member.reshape(-1) for member in members])
    summed = lax.psum_scatter(joined, ("seq", "batch"), scatter_dimension=0, tiled=True)
    whole = lax.all_gather(
        summed.astype(jnp.bfloat16), ("seq", "batch"), axis=0, tiled=True
    ).astype(summed.dtype)
    outputs = []
    offset = 0
    for member in members:
        extent = member.size
        outputs.append(whole[offset : offset + extent].reshape(member.shape))
        offset = offset + extent
    return (
        layer_out,
        input_grad,
        outputs[0],
        outputs[1],
        outputs[2],
        outputs[3],
        outputs[4],
        outputs[5],
        outputs[6],
        outputs[7],
        outputs[8],
        outputs[9],
        outputs[10],
        outputs[11],
    )


def solution(mesh):
    in_specs = (
        P("batch", "seq", None),
        P("batch", "seq", None),
        P("batch", None),
        P(),
        P(),
        P(),
        P(),
        P(),
        P(),
        P(),
        P(),
        P(),
        P(),
        P(),
        P(),
    )
    out_specs = (
        P("batch", "seq", None),
        P("batch", "seq", None),
        P(),
        P(),
        P(),
        P(),
        P(),
        P(),
        P(),
        P(),
        P(),
        P(),
        P(),
        P(),
    )
    return jax.shard_map(
        per_device, mesh=mesh, in_specs=in_specs, out_specs=out_specs, check_vma=False
    )
```

profile of v0, /device:TPU:0, one launch (start us, length us, event | category | flops | bytes accessed | tf_op | source)
XLA Modules:
  0.0 1429.9 jit_solution(15000022725188257302)
XLA Ops:
  20.7 38.8 %all-gather.3.cloned.1.call-done = bf16[1024,768]{1,0:T(8,128)(2,1)} async-done(((bf16[128,768]{1,0:T(8,128)(2,1)}), bf16[1024,768]{1,0:T(8,128)(2,1)}) %all-gather.3.cloned.1.call-update) | async-done | bytes 1572880 | tf_op jit(solution)/shard_map/all_gather | solution.py:133
  59.4 45.8 %all-gather.5.cloned.1.call-done = bf16[1024,768]{1,0:T(8,128)(2,1)} async-done(((bf16[128,768]{1,0:T(8,128)(2,1)}), bf16[1024,768]{1,0:T(8,128)(2,1)}) %all-gather.5.cloned.1.call-update) | async-done | bytes 1572880 | tf_op jit(solution)/shard_map/all_gather | solution.py:134
  105.7 144.0 %while.39 = (s32[]{:T(128)}, f32[12,128]{1,0:T(8,128)}, f32[12,128]{1,0:T(8,128)}, f32[12,128,64]{1,2,0:T(8,128)}, s32[128]{0:T(128)}, /*index=5*/s32[9]{0:T(128...) while((s32[]{:T(128)}, f32[12,128]{1,0:T(8,128)}, ...), condition=%wide.region_8.9_spmd.clone, body=%wide.region_4.8_spmd.clone.sunk | while | flops 54422532 | bytes 5542175 | solution.py:145
  112.7 2.9 select_reduce_fusion.2
  129.9 2.9 select_reduce_fusion.2
  148.0 2.9 select_reduce_fusion.2
  166.1 2.9 select_reduce_fusion.2
  184.2 2.9 select_reduce_fusion.2
  202.3 2.9 select_reduce_fusion.2
  220.4 2.9 select_reduce_fusion.2
  238.6 2.9 select_reduce_fusion.2
  253.0 3.3 convolution_add_fusion.2
  256.4 5.5 convert_reduce_fusion.2
  272.0 215.4 %while.40 = (s32[]{:T(128)}, bf16[128,768]{0,1:T(8,128)(2,1)}, bf16[128,768]{0,1:T(8,128)(2,1)}, f32[128,768]{0,1:T(8,128)}, f32[128,768]{0,1:T(8,128)}, /*index...) while((s32[]{:T(128)}, bf16[128,768]{0,1:T(8,128)(2,1)}, ...), condition=%wide.region_15.16_spmd.clone, body=%wide.region_13.15_spmd.clone.sunk | while | flops 130993680 | bytes 19995340 | solution.py:208
  273.6 3.1 collective-permute-start
  278.3 4.7 collective-permute-start.1
  293.7 5.5 collective-permute-done.2
  321.9 3.9 collective-permute-done.2
  334.8 3.0 collective-permute-start.1
  347.6 4.5 collective-permute-done.2
  386.5 3.6 collective-permute-start.1
  397.0 2.8 collective-permute-start.3
  413.4 3.6 collective-permute-start.1
  427.4 3.9 collective-permute-done.2
  465.6 3.6 collective-permute-start.1
  476.1 2.8 collective-permute-start.3
  493.2 4.2 fusion.60
  499.6 5.3 convolution_bitcast_fusion.1
  504.8 5.2 fusion.51
  510.6 7.9 reshape.357
  520.9 9.6 copy.69
  530.5 10.8 reshape.360
  547.7 60.7 %dynamic-update-slice.3 = f32[7087872]{0:T(1024)} dynamic-update-slice(f32[7087872]{0:T(1024)} %constant_dynamic-update-slice_fusion.8, f32[1769472]{0:T(1024)} %reshape.357, s32[]{} %constant.149) | dynamic-update-slice | bytes 14155780
  609.7 20.3 %dynamic-update-slice.5 = f32[7087872]{0:T(1024)} dynamic-update-slice(f32[7087872]{0:T(1024)} %constant_dynamic-update-slice_fusion.7, f32[589824]{0:T(1024)S(1)} %reshape.358, s32[]{} %constant.151) | dynamic-update-slice | bytes 4718596
  633.9 9.3 constant_dynamic-update-slice_fusion.3
  643.8 3.9 constant_dynamic-update-slice_fusion.1
  648.4 457.8 %all-reduce.6 = bf16[7087872]{0:T(1024)(128)(2,1)} all-reduce(f32[7087872]{0:T(1024)} %constant_dynamic-update-slice_fusion), channel_id=2, replica_groups=mesh['seq'=8,'batch'=4] {'seq','batch'}, use_global_device_ids=true, to_apply=%region_26.27.clone | all-reduce | flops 7087872 | bytes 42527232
  1107.4 5.2 broadcast.252
  1112.7 7.6 dynamic-update-slice
  1121.6 4.1 fusion.35
  1125.7 242.6 %all-reduce.5.cloned.1.call-done = bf16[7087872]{0:T(1024)(128)(2,1)} async-done(((bf16[7087872]{0:T(1024)(128)(2,1)}), bf16[7087872]{0:T(1024)(128)(2,1)}) %all-reduce.5.cloned.1.call-update) | async-done | bytes 14175760
  1368.3 9.6 fusion.69
  1377.9 10.9 reshape.362
  1388.8 11.3 slice.80
  1400.1 4.7 slice.87
  1404.7 8.2 reshape.361
  1413.0 3.0 slice.89
  1416.0 3.4 slice.73
  (567 shorter events, 342.4 us)
Async XLA Ops:
  7.2 52.3 %all-gather.3.cloned.1.call-start = ((), (), s32[]{:S(2)}) async-start(), calls=%async_computation | async-start | bytes 1769472 | tf_op jit(solution)/shard_map/all_gather | solution.py:133
  12.6 92.6 %all-gather.5.cloned.1.call-start = ((), (), s32[]{:S(2)}) async-start(), calls=%async_computation.1 | async-start | bytes 1769472 | tf_op jit(solution)/shard_map/all_gather | solution.py:134
  13.4 1354.9 %all-reduce.5.cloned.1.call-start = ((), (), s32[]{:S(2)}) async-start(), calls=%async_computation.2 | async-start | bytes 28352512
  252.7 11.5 copy-start.4
  272.0 13.9 copy-start.48
  272.0 13.9 copy-start.49
  273.6 29.4 %collective-permute-start = (bf16[128,768]{0,1:T(8,128)(2,1)}, bf16[128,768]{0,1:T(8,128)(2,1)}, u32[]{:S(2)}, u32[]{:S(2)}) collective-permute-start(bf16[128,768]{0,1:T(8,128)(2,1)} %copy.93), channel_id=1, source_target_pairs={{0,4},{4,8},{8,12},{12,16},{16,20},{20,24},{24,28},{1,5},{5,9},{9,... | collective-permute-start | bytes 589832 | tf_op jit(solution)/shard_map/while/body/eval_jaxpr/ppermute | solution.py:16
  278.3 24.7 %collective-permute-start.1 = (bf16[128,768]{0,1:T(8,128)(2,1)}, bf16[128,768]{0,1:T(8,128)(2,1)}, u32[]{:S(2)}, u32[]{:S(2)}) collective-permute-start(bf16[128,768]{0,1:T(8,128)(2,1)} %copy.94), channel_id=1, source_target_pairs={{0,4},{4,8},{8,12},{12,16},{16,20},{20,24},{24,28},{1,5},{5,9},{9,... | collective-permute-start | bytes 589832 | tf_op jit(solution)/shard_map/while/body/eval_jaxpr/ppermute | solution.py:16
  288.7 10.5 collective-permute-start.2
  290.0 11.3 collective-permute-start.3
  304.7 24.9 %collective-permute-start = (bf16[128,768]{0,1:T(8,128)(2,1)}, bf16[128,768]{0,1:T(8,128)(2,1)}, u32[]{:S(2)}, u32[]{:S(2)}) collective-permute-start(bf16[128,768]{0,1:T(8,128)(2,1)} %copy.93), channel_id=1, source_target_pairs={{0,4},{4,8},{8,12},{12,16},{16,20},{20,24},{24,28},{1,5},{5,9},{9,... | collective-permute-start | bytes 589832 | tf_op jit(solution)/shard_map/while/body/eval_jaxpr/ppermute | solution.py:16
  308.2 21.4 %collective-permute-start.1 = (bf16[128,768]{0,1:T(8,128)(2,1)}, bf16[128,768]{0,1:T(8,128)(2,1)}, u32[]{:S(2)}, u32[]{:S(2)}) collective-permute-start(bf16[128,768]{0,1:T(8,128)(2,1)} %copy.94), channel_id=1, source_target_pairs={{0,4},{4,8},{8,12},{12,16},{16,20},{20,24},{24,28},{1,5},{5,9},{9,... | collective-permute-start | bytes 589832 | tf_op jit(solution)/shard_map/while/body/eval_jaxpr/ppermute | solution.py:16
  316.5 9.3 collective-permute-start.2
  317.8 10.1 collective-permute-start.3
  331.2 24.7 %collective-permute-start = (bf16[128,768]{0,1:T(8,128)(2,1)}, bf16[128,768]{0,1:T(8,128)(2,1)}, u32[]{:S(2)}, u32[]{:S(2)}) collective-permute-start(bf16[128,768]{0,1:T(8,128)(2,1)} %copy.93), channel_id=1, source_target_pairs={{0,4},{4,8},{8,12},{12,16},{16,20},{20,24},{24,28},{1,5},{5,9},{9,... | collective-permute-start | bytes 589832 | tf_op jit(solution)/shard_map/while/body/eval_jaxpr/ppermute | solution.py:16
  334.8 21.1 %collective-permute-start.1 = (bf16[128,768]{0,1:T(8,128)(2,1)}, bf16[128,768]{0,1:T(8,128)(2,1)}, u32[]{:S(2)}, u32[]{:S(2)}) collective-permute-start(bf16[128,768]{0,1:T(8,128)(2,1)} %copy.94), channel_id=1, source_target_pairs={{0,4},{4,8},{8,12},{12,16},{16,20},{20,24},{24,28},{1,5},{5,9},{9,... | collective-permute-start | bytes 589832 | tf_op jit(solution)/shard_map/while/body/eval_jaxpr/ppermute | solution.py:16
  343.4 8.7 collective-permute-start.2
  344.8 9.5 collective-permute-start.3
  357.6 23.7 %collective-permute-start = (bf16[128,768]{0,1:T(8,128)(2,1)}, bf16[128,768]{0,1:T(8,128)(2,1)}, u32[]{:S(2)}, u32[]{:S(2)}) collective-permute-start(bf16[128,768]{0,1:T(8,128)(2,1)} %copy.93), channel_id=1, source_target_pairs={{0,4},{4,8},{8,12},{12,16},{16,20},{20,24},{24,28},{1,5},{5,9},{9,... | collective-permute-start | bytes 589832 | tf_op jit(solution)/shard_map/while/body/eval_jaxpr/ppermute | solution.py:16
  361.1 20.1 %collective-permute-start.1 = (bf16[128,768]{0,1:T(8,128)(2,1)}, bf16[128,768]{0,1:T(8,128)(2,1)}, u32[]{:S(2)}, u32[]{:S(2)}) collective-permute-start(bf16[128,768]{0,1:T(8,128)(2,1)} %copy.94), channel_id=1, source_target_pairs={{0,4},{4,8},{8,12},{12,16},{16,20},{20,24},{24,28},{1,5},{5,9},{9,... | collective-permute-start | bytes 589832 | tf_op jit(solution)/shard_map/while/body/eval_jaxpr/ppermute | solution.py:16
  368.7 8.7 collective-permute-start.2
  370.1 9.5 collective-permute-start.3
  381.2 11.6 copy-start.48
  381.2 11.6 copy-start.49
  382.9 25.3 %collective-permute-start = (bf16[128,768]{0,1:T(8,128)(2,1)}, bf16[128,768]{0,1:T(8,128)(2,1)}, u32[]{:S(2)}, u32[]{:S(2)}) collective-permute-start(bf16[128,768]{0,1:T(8,128)(2,1)} %copy.93), channel_id=1, source_target_pairs={{0,4},{4,8},{8,12},{12,16},{16,20},{20,24},{24,28},{1,5},{5,9},{9,... | collective-permute-start | bytes 589832 | tf_op jit(solution)/shard_map/while/body/eval_jaxpr/ppermute | solution.py:16
  386.5 21.7 %collective-permute-start.1 = (bf16[128,768]{0,1:T(8,128)(2,1)}, bf16[128,768]{0,1:T(8,128)(2,1)}, u32[]{:S(2)}, u32[]{:S(2)}) collective-permute-start(bf16[128,768]{0,1:T(8,128)(2,1)} %copy.94), channel_id=1, source_target_pairs={{0,4},{4,8},{8,12},{12,16},{16,20},{20,24},{24,28},{1,5},{5,9},{9,... | collective-permute-start | bytes 589832 | tf_op jit(solution)/shard_map/while/body/eval_jaxpr/ppermute | solution.py:16
  395.6 8.7 collective-permute-start.2
  397.0 9.5 collective-permute-start.3
  408.1 11.7 copy-start.48
  408.1 11.7 copy-start.49
  409.8 25.3 %collective-permute-start = (bf16[128,768]{0,1:T(8,128)(2,1)}, bf16[128,768]{0,1:T(8,128)(2,1)}, u32[]{:S(2)}, u32[]{:S(2)}) collective-permute-start(bf16[128,768]{0,1:T(8,128)(2,1)} %copy.93), channel_id=1, source_target_pairs={{0,4},{4,8},{8,12},{12,16},{16,20},{20,24},{24,28},{1,5},{5,9},{9,... | collective-permute-start | bytes 589832 | tf_op jit(solution)/shard_map/while/body/eval_jaxpr/ppermute | solution.py:16
  413.4 21.7 %collective-permute-start.1 = (bf16[128,768]{0,1:T(8,128)(2,1)}, bf16[128,768]{0,1:T(8,128)(2,1)}, u32[]{:S(2)}, u32[]{:S(2)}) collective-permute-start(bf16[128,768]{0,1:T(8,128)(2,1)} %copy.94), channel_id=1, source_target_pairs={{0,4},{4,8},{8,12},{12,16},{16,20},{20,24},{24,28},{1,5},{5,9},{9,... | collective-permute-start | bytes 589832 | tf_op jit(solution)/shard_map/while/body/eval_jaxpr/ppermute | solution.py:16
  422.6 8.7 collective-permute-start.2
  423.9 9.5 collective-permute-start.3
  436.7 23.7 %collective-permute-start = (bf16[128,768]{0,1:T(8,128)(2,1)}, bf16[128,768]{0,1:T(8,128)(2,1)}, u32[]{:S(2)}, u32[]{:S(2)}) collective-permute-start(bf16[128,768]{0,1:T(8,128)(2,1)} %copy.93), channel_id=1, source_target_pairs={{0,4},{4,8},{8,12},{12,16},{16,20},{20,24},{24,28},{1,5},{5,9},{9,... | collective-permute-start | bytes 589832 | tf_op jit(solution)/shard_map/while/body/eval_jaxpr/ppermute | solution.py:16
  440.3 20.1 %collective-permute-start.1 = (bf16[128,768]{0,1:T(8,128)(2,1)}, bf16[128,768]{0,1:T(8,128)(2,1)}, u32[]{:S(2)}, u32[]{:S(2)}) collective-permute-start(bf16[128,768]{0,1:T(8,128)(2,1)} %copy.94), channel_id=1, source_target_pairs={{0,4},{4,8},{8,12},{12,16},{16,20},{20,24},{24,28},{1,5},{5,9},{9,... | collective-permute-start | bytes 589832 | tf_op jit(solution)/shard_map/while/body/eval_jaxpr/ppermute | solution.py:16
  447.9 8.7 collective-permute-start.2
  449.2 9.5 collective-permute-start.3
  460.4 11.6 copy-start.48
  460.4 11.6 copy-start.49
  462.0 25.3 %collective-permute-start = (bf16[128,768]{0,1:T(8,128)(2,1)}, bf16[128,768]{0,1:T(8,128)(2,1)}, u32[]{:S(2)}, u32[]{:S(2)}) collective-permute-start(bf16[128,768]{0,1:T(8,128)(2,1)} %copy.93), channel_id=1, source_target_pairs={{0,4},{4,8},{8,12},{12,16},{16,20},{20,24},{24,28},{1,5},{5,9},{9,... | collective-permute-start | bytes 589832 | tf_op jit(solution)/shard_map/while/body/eval_jaxpr/ppermute | solution.py:16
  465.6 21.7 %collective-permute-start.1 = (bf16[128,768]{0,1:T(8,128)(2,1)}, bf16[128,768]{0,1:T(8,128)(2,1)}, u32[]{:S(2)}, u32[]{:S(2)}) collective-permute-start(bf16[128,768]{0,1:T(8,128)(2,1)} %copy.94), channel_id=1, source_target_pairs={{0,4},{4,8},{8,12},{12,16},{16,20},{20,24},{24,28},{1,5},{5,9},{9,... | collective-permute-start | bytes 589832 | tf_op jit(solution)/shard_map/while/body/eval_jaxpr/ppermute | solution.py:16
  474.8 8.7 collective-permute-start.2
  476.1 9.5 collective-permute-start.3
  530.5 12.1 copy-start.15
  609.7 20.3 %copy-start.40 = (f32[768]{0:T(1024)S(1)}, f32[768]{0:T(1024)}, u32[]{:S(2)}) copy-start(f32[768]{0:T(1024)} %get-tuple-element.658) | copy-start | bytes 9220
  609.7 21.6 %copy-start.39 = (f32[768]{0:T(1024)S(1)}, f32[768]{0:T(1024)}, u32[]{:S(2)}) copy-start(f32[768]{0:T(1024)} %get-tuple-element.599) | copy-start | bytes 9220
  609.7 22.9 %copy-start.38 = (f32[768]{0:T(1024)S(1)}, f32[768]{0:T(1024)}, u32[]{:S(2)}) copy-start(f32[768]{0:T(1024)} %get-tuple-element.603) | copy-start | bytes 9220
  (104 other events, 413.6 us)
Sparse Core Ops, SparseCore 0:
  12.8 46.6 all-gather.2
  62.2 42.9 all-gather.4
  1120.4 247.8 all-reduce.4
where the time goes:
time: 1440 us; the launch traced here: 1430 us
  blocking collectives  458 us (32%)
  waiting for transfers between devices  358 us (25%)
  local copies, waits for them, and re-layouts  299 us (21%)
  matrix products  131 us (9%)
  other arithmetic  106 us (7%)
  starting transfers between devices  58.3 us (4%)
    unnamed x1, blocking collectives  458 us
    unnamed x4, waiting for transfers between devices  243 us
    unnamed x123, local copies, waits for them, and re-layouts  133 us
    all_gather x1, waiting for transfers between devices, per_device(): v_all = lax.all_gather(v_flat, 'seq', axis=0, tiled=True)  45.8 us
    ppermute x16, starting transfers between devices, from_behind(): return lax.ppermute(shard, axis, pairs)  41.9 us
    all_gather x1, waiting for transfers between devices, per_device(): k_all = lax.all_gather(k_flat, 'seq', axis=0, tiled=True)  38.8 us
    slice x8, local copies, waits for them, and re-layouts, per_device(): outputs.append(whole[offset:offset + extent].reshape(member.shape))  35.9 us
    dot_general x16, matrix products, scores_of(): jnp.einsum('qhd,khd->hqk', q_heads, k_heads, preferred_element_type=jnp.f...  33.6 us
  transfers between devices with their start and end apart: 35, of which 19 were waited for; matrix products, arithmetic and copies ran while one was open for 9% of the time, Pallas kernels for 0%

commit v1 on v0

--- a/solution.py
+++ b/solution.py
@@ -8,6 +8,12 @@
 HD = 64
 norm_eps = 1e-05
 masked_low = -1e30
+
+
+def use_vector(row_data, z_in):
+    r_now = jnp.concatenate([row_data, z_in], axis=1)
+    built = jax.lax.all_gather(r_now, "seq", axis=0, tiled=True)
+    return jnp.split(built, [row_data.shape[1]], axis=1)
 
 
 def from_behind(shard, axis, by):
@@ -130,8 +136,7 @@
         jnp.zeros((HEADS, rows, HD), jnp.float32),
     )
     state = start_state
-    k_all = lax.all_gather(k_flat, "seq", axis=0, tiled=True)
-    v_all = lax.all_gather(v_flat, "seq", axis=0, tiled=True)
+    k_all, v_all = use_vector(k_flat, v_flat)
     fold_extent = k_all.shape[0]
     number = fold_extent // rows
 

time: 1440 us -> 1420 us (0.986)
  waiting for transfers between devices: 358 us -> 325 us
    all_gather x2 -> x1, waiting for transfers between devices: 84.5 us -> 54 us  [use_vector(): built = jax.lax.all_gather(r_now, 'seq', axis=0, tiled=True)]
    unnamed x123 -> x125, local copies, waits for them, and re-layouts: 133 us -> 134 us
    unnamed x4 -> x3, waiting for transfers between devices: 243 us -> 243 us
  transfers between devices with their start and end apart: 35 -> 34, of which waited for: 19 -> 18; matrix products, arithmetic and copies ran while one was open for 9% -> 9% of each run, Pallas kernels for 0% -> 0%
where the time goes in v1:
time: 1420 us; the launch traced here: 1410 us
  blocking collectives  458 us (32%)
  waiting for transfers between devices  325 us (23%)
  local copies, waits for them, and re-layouts  305 us (21%)
  matrix products  131 us (9%)
  other arithmetic  107 us (8%)
  starting transfers between devices  59.1 us (4%)
  between operations  14.6 us (1%)
    unnamed x1, blocking collectives  458 us
    unnamed x3, waiting for transfers between devices  243 us
    unnamed x125, local copies, waits for them, and re-layouts  134 us
    all_gather x1, waiting for transfers between devices, use_vector(): built = jax.lax.all_gather(r_now, 'seq', axis=0, tiled=True)  54 us
    ppermute x16, starting transfers between devices, from_behind(): return lax.ppermute(shard, axis, pairs)  42.1 us
    slice x8, local copies, waits for them, and re-layouts, per_device(): outputs.append(whole[offset:offset + extent].reshape(member.shape))  35.9 us
    dot_general x16, matrix products, scores_of(): jnp.einsum('qhd,khd->hqk', q_heads, k_heads, preferred_element_type=jnp.f...  33.6 us
    while x152, local copies, waits for them, and re-layouts  31.6 us
  transfers between devices with their start and end apart: 34, of which 18 were waited for; matrix products, arithmetic and copies ran while one was open for 9% of the time, Pallas kernels for 0%

profile of v1, /device:TPU:0, one launch (start us, length us, event | category | flops | bytes accessed | tf_op | source)
XLA Modules:
  0.0 1405.8 jit_solution(11683303396505635094)
XLA Ops:
  22.7 54.0 %all-gather.2.cloned.1.call-done = bf16[1024,1536]{1,0:T(8,128)(2,1)} async-done(((bf16[128,1536]{1,0:T(8,128)(2,1)}), bf16[1024,1536]{1,0:T(8,128)(2,1)}) %all-gather.2.cloned.1.call-update) | async-done | bytes 3145744 | tf_op jit(solution)/shard_map/all_gather | solution.py:15
  76.7 3.7 fusion.70
  81.0 144.4 %while.39 = (s32[]{:T(128)}, f32[12,128]{1,0:T(8,128)}, f32[12,128]{1,0:T(8,128)}, f32[12,128,64]{1,2,0:T(8,128)}, s32[128]{0:T(128)}, /*index=5*/s32[9]{0:T(128...) while((s32[]{:T(128)}, f32[12,128]{1,0:T(8,128)}, ...), condition=%wide.region_8.9_spmd.clone, body=%wide.region_4.8_spmd.clone.sunk | while | flops 54422532 | bytes 5542175 | solution.py:150
  87.9 2.9 select_reduce_fusion.2
  105.2 2.9 select_reduce_fusion.2
  123.4 2.9 select_reduce_fusion.2
  141.5 2.9 select_reduce_fusion.2
  159.7 2.9 select_reduce_fusion.2
  177.8 2.9 select_reduce_fusion.2
  196.0 2.9 select_reduce_fusion.2
  214.2 2.9 select_reduce_fusion.2
  228.6 3.3 convolution_add_fusion.2
  232.0 5.5 convert_reduce_fusion.2
  247.6 215.2 %while.40 = (s32[]{:T(128)}, bf16[128,768]{0,1:T(8,128)(2,1)}, bf16[128,768]{0,1:T(8,128)(2,1)}, f32[128,768]{0,1:T(8,128)}, f32[128,768]{0,1:T(8,128)}, /*index...) while((s32[]{:T(128)}, bf16[128,768]{0,1:T(8,128)(2,1)}, ...), condition=%wide.region_15.16_spmd.clone, body=%wide.region_13.15_spmd.clone.sunk | while | flops 130993680 | bytes 19995340 | solution.py:213
  249.2 3.1 collective-permute-start
  254.0 4.3 collective-permute-start.1
  269.2 4.6 collective-permute-done.2
  282.9 3.2 collective-permute-start.1
  297.5 3.3 collective-permute-done.2
  309.8 3.7 collective-permute-start.1
  323.2 4.6 collective-permute-done.2
  362.1 3.2 collective-permute-start.1
  372.7 2.8 collective-permute-start.3
  389.0 3.7 collective-permute-start.1
  403.2 3.9 collective-permute-done.2
  441.4 3.2 collective-permute-start.1
  468.6 4.2 fusion.60
  475.0 5.3 convolution_bitcast_fusion.1
  480.3 5.2 fusion.51
  486.1 7.9 reshape.357
  496.3 9.6 copy.69
  506.0 10.8 reshape.360
  523.2 60.8 %dynamic-update-slice.3 = f32[7087872]{0:T(1024)} dynamic-update-slice(f32[7087872]{0:T(1024)} %constant_dynamic-update-slice_fusion.8, f32[1769472]{0:T(1024)} %reshape.357, s32[]{} %constant.149) | dynamic-update-slice | bytes 14155780
  585.3 20.3 %dynamic-update-slice.5 = f32[7087872]{0:T(1024)} dynamic-update-slice(f32[7087872]{0:T(1024)} %constant_dynamic-update-slice_fusion.7, f32[589824]{0:T(1024)S(1)} %reshape.358, s32[]{} %constant.151) | dynamic-update-slice | bytes 4718596
  609.5 9.3 constant_dynamic-update-slice_fusion.3
  619.4 3.9 constant_dynamic-update-slice_fusion.1
  623.9 457.8 %all-reduce.6 = bf16[7087872]{0:T(1024)(128)(2,1)} all-reduce(f32[7087872]{0:T(1024)} %constant_dynamic-update-slice_fusion), channel_id=2, replica_groups=mesh['seq'=8,'batch'=4] {'seq','batch'}, use_global_device_ids=true, to_apply=%region_26.27.clone | all-reduce | flops 7087872 | bytes 42527232
  1083.0 5.3 broadcast.252
  1088.2 7.6 dynamic-update-slice
  1097.2 4.1 fusion.35
  1101.3 242.7 %all-reduce.5.cloned.1.call-done = bf16[7087872]{0:T(1024)(128)(2,1)} async-done(((bf16[7087872]{0:T(1024)(128)(2,1)}), bf16[7087872]{0:T(1024)(128)(2,1)}) %all-reduce.5.cloned.1.call-update) | async-done | bytes 14175760
  1344.0 9.6 fusion.69
  1353.6 10.9 reshape.362
  1364.5 11.3 slice.81
  1375.7 4.6 slice.88
  1380.4 8.2 reshape.361
  1388.6 3.0 slice.90
  1391.7 3.4 slice.74
  (568 shorter events, 346.0 us)
Async XLA Ops:
  7.2 69.5 %all-gather.2.cloned.1.call-start = ((), (), s32[]{:S(2)}) async-start(), calls=%async_computation | async-start | bytes 3538944 | tf_op jit(solution)/shard_map/all_gather | solution.py:15
  13.4 1330.6 %all-reduce.5.cloned.1.call-start = ((), (), s32[]{:S(2)}) async-start(), calls=%async_computation.1 | async-start | bytes 28352512
  228.3 11.5 copy-start.4
  228.3 11.5 copy-start.37
  247.6 13.5 copy-start.49
  247.6 13.5 copy-start.50
  249.2 28.4 %collective-permute-start = (bf16[128,768]{0,1:T(8,128)(2,1)}, bf16[128,768]{0,1:T(8,128)(2,1)}, u32[]{:S(2)}, u32[]{:S(2)}) collective-permute-start(bf16[128,768]{0,1:T(8,128)(2,1)} %copy.93), channel_id=1, source_target_pairs={{0,4},{4,8},{8,12},{12,16},{16,20},{20,24},{24,28},{1,5},{5,9},{9,... | collective-permute-start | bytes 589832 | tf_op jit(solution)/shard_map/while/body/eval_jaxpr/ppermute | solution.py:22
  254.0 23.7 %collective-permute-start.1 = (bf16[128,768]{0,1:T(8,128)(2,1)}, bf16[128,768]{0,1:T(8,128)(2,1)}, u32[]{:S(2)}, u32[]{:S(2)}) collective-permute-start(bf16[128,768]{0,1:T(8,128)(2,1)} %copy.94), channel_id=1, source_target_pairs={{0,4},{4,8},{8,12},{12,16},{16,20},{20,24},{24,28},{1,5},{5,9},{9,... | collective-permute-start | bytes 589832 | tf_op jit(solution)/shard_map/while/body/eval_jaxpr/ppermute | solution.py:22
  263.9 10.0 collective-permute-start.2
  265.2 10.8 collective-permute-start.3
  279.3 25.2 %collective-permute-start = (bf16[128,768]{0,1:T(8,128)(2,1)}, bf16[128,768]{0,1:T(8,128)(2,1)}, u32[]{:S(2)}, u32[]{:S(2)}) collective-permute-start(bf16[128,768]{0,1:T(8,128)(2,1)} %copy.93), channel_id=1, source_target_pairs={{0,4},{4,8},{8,12},{12,16},{16,20},{20,24},{24,28},{1,5},{5,9},{9,... | collective-permute-start | bytes 589832 | tf_op jit(solution)/shard_map/while/body/eval_jaxpr/ppermute | solution.py:22
  282.9 21.7 %collective-permute-start.1 = (bf16[128,768]{0,1:T(8,128)(2,1)}, bf16[128,768]{0,1:T(8,128)(2,1)}, u32[]{:S(2)}, u32[]{:S(2)}) collective-permute-start(bf16[128,768]{0,1:T(8,128)(2,1)} %copy.94), channel_id=1, source_target_pairs={{0,4},{4,8},{8,12},{12,16},{16,20},{20,24},{24,28},{1,5},{5,9},{9,... | collective-permute-start | bytes 589832 | tf_op jit(solution)/shard_map/while/body/eval_jaxpr/ppermute | solution.py:22
  291.7 9.0 collective-permute-start.2
  293.0 9.8 collective-permute-start.3
  304.6 11.7 copy-start.49
  304.6 11.7 copy-start.50
  306.2 25.4 %collective-permute-start = (bf16[128,768]{0,1:T(8,128)(2,1)}, bf16[128,768]{0,1:T(8,128)(2,1)}, u32[]{:S(2)}, u32[]{:S(2)}) collective-permute-start(bf16[128,768]{0,1:T(8,128)(2,1)} %copy.93), channel_id=1, source_target_pairs={{0,4},{4,8},{8,12},{12,16},{16,20},{20,24},{24,28},{1,5},{5,9},{9,... | collective-permute-start | bytes 589832 | tf_op jit(solution)/shard_map/while/body/eval_jaxpr/ppermute | solution.py:22
  309.8 21.8 %collective-permute-start.1 = (bf16[128,768]{0,1:T(8,128)(2,1)}, bf16[128,768]{0,1:T(8,128)(2,1)}, u32[]{:S(2)}, u32[]{:S(2)}) collective-permute-start(bf16[128,768]{0,1:T(8,128)(2,1)} %copy.94), channel_id=1, source_target_pairs={{0,4},{4,8},{8,12},{12,16},{16,20},{20,24},{24,28},{1,5},{5,9},{9,... | collective-permute-start | bytes 589832 | tf_op jit(solution)/shard_map/while/body/eval_jaxpr/ppermute | solution.py:22
  319.1 8.7 collective-permute-start.2
  320.4 9.5 collective-permute-start.3
  333.2 23.7 %collective-permute-start = (bf16[128,768]{0,1:T(8,128)(2,1)}, bf16[128,768]{0,1:T(8,128)(2,1)}, u32[]{:S(2)}, u32[]{:S(2)}) collective-permute-start(bf16[128,768]{0,1:T(8,128)(2,1)} %copy.93), channel_id=1, source_target_pairs={{0,4},{4,8},{8,12},{12,16},{16,20},{20,24},{24,28},{1,5},{5,9},{9,... | collective-permute-start | bytes 589832 | tf_op jit(solution)/shard_map/while/body/eval_jaxpr/ppermute | solution.py:22
  336.8 20.1 %collective-permute-start.1 = (bf16[128,768]{0,1:T(8,128)(2,1)}, bf16[128,768]{0,1:T(8,128)(2,1)}, u32[]{:S(2)}, u32[]{:S(2)}) collective-permute-start(bf16[128,768]{0,1:T(8,128)(2,1)} %copy.94), channel_id=1, source_target_pairs={{0,4},{4,8},{8,12},{12,16},{16,20},{20,24},{24,28},{1,5},{5,9},{9,... | collective-permute-start | bytes 589832 | tf_op jit(solution)/shard_map/while/body/eval_jaxpr/ppermute | solution.py:22
  344.4 8.7 collective-permute-start.2
  345.7 9.5 collective-permute-start.3
  356.9 11.3 copy-start.50
  358.6 24.9 %collective-permute-start = (bf16[128,768]{0,1:T(8,128)(2,1)}, bf16[128,768]{0,1:T(8,128)(2,1)}, u32[]{:S(2)}, u32[]{:S(2)}) collective-permute-start(bf16[128,768]{0,1:T(8,128)(2,1)} %copy.93), channel_id=1, source_target_pairs={{0,4},{4,8},{8,12},{12,16},{16,20},{20,24},{24,28},{1,5},{5,9},{9,... | collective-permute-start | bytes 589832 | tf_op jit(solution)/shard_map/while/body/eval_jaxpr/ppermute | solution.py:22
  362.1 21.4 %collective-permute-start.1 = (bf16[128,768]{0,1:T(8,128)(2,1)}, bf16[128,768]{0,1:T(8,128)(2,1)}, u32[]{:S(2)}, u32[]{:S(2)}) collective-permute-start(bf16[128,768]{0,1:T(8,128)(2,1)} %copy.94), channel_id=1, source_target_pairs={{0,4},{4,8},{8,12},{12,16},{16,20},{20,24},{24,28},{1,5},{5,9},{9,... | collective-permute-start | bytes 589832 | tf_op jit(solution)/shard_map/while/body/eval_jaxpr/ppermute | solution.py:22
  371.0 8.7 collective-permute-start.2
  372.7 9.1 collective-permute-start.3
  383.5 12.1 copy-start.49
  383.5 12.1 copy-start.50
  385.1 25.7 %collective-permute-start = (bf16[128,768]{0,1:T(8,128)(2,1)}, bf16[128,768]{0,1:T(8,128)(2,1)}, u32[]{:S(2)}, u32[]{:S(2)}) collective-permute-start(bf16[128,768]{0,1:T(8,128)(2,1)} %copy.93), channel_id=1, source_target_pairs={{0,4},{4,8},{8,12},{12,16},{16,20},{20,24},{24,28},{1,5},{5,9},{9,... | collective-permute-start | bytes 589832 | tf_op jit(solution)/shard_map/while/body/eval_jaxpr/ppermute | solution.py:22
  389.0 21.8 %collective-permute-start.1 = (bf16[128,768]{0,1:T(8,128)(2,1)}, bf16[128,768]{0,1:T(8,128)(2,1)}, u32[]{:S(2)}, u32[]{:S(2)}) collective-permute-start(bf16[128,768]{0,1:T(8,128)(2,1)} %copy.94), channel_id=1, source_target_pairs={{0,4},{4,8},{8,12},{12,16},{16,20},{20,24},{24,28},{1,5},{5,9},{9,... | collective-permute-start | bytes 589832 | tf_op jit(solution)/shard_map/while/body/eval_jaxpr/ppermute | solution.py:22
  398.4 8.7 collective-permute-start.2
  399.7 9.5 collective-permute-start.3
  412.5 23.7 %collective-permute-start = (bf16[128,768]{0,1:T(8,128)(2,1)}, bf16[128,768]{0,1:T(8,128)(2,1)}, u32[]{:S(2)}, u32[]{:S(2)}) collective-permute-start(bf16[128,768]{0,1:T(8,128)(2,1)} %copy.93), channel_id=1, source_target_pairs={{0,4},{4,8},{8,12},{12,16},{16,20},{20,24},{24,28},{1,5},{5,9},{9,... | collective-permute-start | bytes 589832 | tf_op jit(solution)/shard_map/while/body/eval_jaxpr/ppermute | solution.py:22
  416.1 20.1 %collective-permute-start.1 = (bf16[128,768]{0,1:T(8,128)(2,1)}, bf16[128,768]{0,1:T(8,128)(2,1)}, u32[]{:S(2)}, u32[]{:S(2)}) collective-permute-start(bf16[128,768]{0,1:T(8,128)(2,1)} %copy.94), channel_id=1, source_target_pairs={{0,4},{4,8},{8,12},{12,16},{16,20},{20,24},{24,28},{1,5},{5,9},{9,... | collective-permute-start | bytes 589832 | tf_op jit(solution)/shard_map/while/body/eval_jaxpr/ppermute | solution.py:22
  423.7 8.7 collective-permute-start.2
  425.0 9.5 collective-permute-start.3
  436.2 11.3 copy-start.50
  437.8 24.9 %collective-permute-start = (bf16[128,768]{0,1:T(8,128)(2,1)}, bf16[128,768]{0,1:T(8,128)(2,1)}, u32[]{:S(2)}, u32[]{:S(2)}) collective-permute-start(bf16[128,768]{0,1:T(8,128)(2,1)} %copy.93), channel_id=1, source_target_pairs={{0,4},{4,8},{8,12},{12,16},{16,20},{20,24},{24,28},{1,5},{5,9},{9,... | collective-permute-start | bytes 589832 | tf_op jit(solution)/shard_map/while/body/eval_jaxpr/ppermute | solution.py:22
  441.4 21.4 %collective-permute-start.1 = (bf16[128,768]{0,1:T(8,128)(2,1)}, bf16[128,768]{0,1:T(8,128)(2,1)}, u32[]{:S(2)}, u32[]{:S(2)}) collective-permute-start(bf16[128,768]{0,1:T(8,128)(2,1)} %copy.94), channel_id=1, source_target_pairs={{0,4},{4,8},{8,12},{12,16},{16,20},{20,24},{24,28},{1,5},{5,9},{9,... | collective-permute-start | bytes 589832 | tf_op jit(solution)/shard_map/while/body/eval_jaxpr/ppermute | solution.py:22
  450.3 8.7 collective-permute-start.2
  451.9 9.1 collective-permute-start.3
  506.0 12.1 copy-start.16
  585.3 20.3 %copy-start.41 = (f32[768]{0:T(1024)S(1)}, f32[768]{0:T(1024)}, u32[]{:S(2)}) copy-start(f32[768]{0:T(1024)} %get-tuple-element.658) | copy-start | bytes 9220
  585.3 21.6 %copy-start.40 = (f32[768]{0:T(1024)S(1)}, f32[768]{0:T(1024)}, u32[]{:S(2)}) copy-start(f32[768]{0:T(1024)} %get-tuple-element.599) | copy-start | bytes 9220
  585.3 22.9 %copy-start.39 = (f32[768]{0:T(1024)S(1)}, f32[768]{0:T(1024)}, u32[]{:S(2)}) copy-start(f32[768]{0:T(1024)} %get-tuple-element.603) | copy-start | bytes 9220
  (104 other events, 404.2 us)
Sparse Core Ops, SparseCore 0:
  13.5 63.1 all-gather.1
  1096.0 247.9 all-reduce.4
